TPU v7x, 32 devices: a whole 2x2x4 slice. The times are simulated.
32 devices in a mesh: seq: 8 (over z, y), tp: 4 (over x, core).
Axes of the slice: x: 2, y: 2, z: 4, core: 2. Of those that a mesh axis runs over, the one named last changes fastest.
Arguments:
- image_rows: bfloat16 [1024, 1280], P('seq'), may hold values from -6 to 6
- norm_gain: float32 [1280], replicated, may hold values from 0.1 to 1.9
- expand_weight: bfloat16 [1280, 5120], P(None, 'tp'), may hold values from -0.15625 to 0.15625
- shrink_weight: bfloat16 [5120, 1280], P('tp'), may hold values from -0.078125 to 0.078125
- projector: bfloat16 [1280, 8192], P(None, 'tp'), may hold values from -0.15625 to 0.15625
- kv_weight: bfloat16 [8192, 2048], P('tp', 'seq'), may hold values from -0.0625 to 0.0625
- queries: bfloat16 [2048, 8192], P('seq', 'tp'), may hold values from -240 to 240
- send_list: int32 [8, 8, 32], P('seq'), may hold values from -1 to 127, as said below
- block_mask: int32 [16, 4], P('seq'), may hold values from 0 to 1, as said below
Outputs:
- states: bfloat16 [1024, 8192], P('seq', 'tp')
- context: bfloat16 [2048, 8192], P('seq', 'tp')
Inputs may be any that keep to these rules, and one draw needn't show every extreme that they name: `send_list`: each sequence shard belongs to one document, whose text fills a run of whole sequence shards, and references that document's one image of 1 to 4 tiles; each draw has a document of one tile and one of 4. The image's 32 rows on encoder shard s form a run of consecutive local rows, named in order and alike for every sequence shard of the document; slot s * 32 + c is live exactly when it is below 64 times the image's tile count, else -1. block_mask[b, q] is 1 exactly when tile q is among the tiles of the image of block b's document and block b does not precede that image; at most the first block of a document precedes it. So a seen slot is always live.
All inputs are finite; a program needn't handle non-finite values.
Results may differ from a plain program's by a relative error of at most 0.03.
Values may be sent and summed in bfloat16 or wider, within the bound.
A program may use at most 64 MiB of HBM per device.

v0:
```python
import math

import jax
import jax.numpy as jnp
from jax import lax
from jax.experimental import pallas as pl
from jax.experimental.pallas import tpu as pltpu
from jax.sharding import PartitionSpec as P

HDIM = 128
MAX_TILES = 4
QBLK = 128


def layer_norm(row_data, norm_gain):
    values = row_data.astype(jnp.float32)
    center = values - jnp.mean(values, axis=1, keepdims=True)
    spread = jnp.mean(center * center, axis=1, keepdims=True)
    return (center * lax.rsqrt(spread + 1e-05) * norm_gain).astype(jnp.bfloat16)


def select_rows(row_data, wanted):
    flat = wanted.reshape(-1)
    hot = (flat[:, None] == jnp.arange(row_data.shape[0], dtype=jnp.int32)[None, :]).astype(jnp.bfloat16)
    picked = jnp.dot(hot, row_data, preferred_element_type=jnp.float32).astype(jnp.bfloat16)
    return picked.reshape(wanted.shape + (row_data.shape[1],))


def attend_kernel(mask_ref, q_ref, kv_ref, o_ref):
    tokens, width = q_ref.shape
    slots = kv_ref.shape[0]
    groups = kv_ref.shape[1] // (2 * HDIM)
    per_group = width // (groups * HDIM)
    tile_rows = slots // MAX_TILES
    scale = 1.0 / math.sqrt(HDIM)
    blocks = mask_ref.shape[0]
    slot = lax.broadcasted_iota(jnp.int32, (QBLK, slots), 1)
    for b in range(blocks):
        seen = jnp.zeros((QBLK, slots), jnp.float32)
        for tile in range(MAX_TILES):
            inside = (slot >= tile * tile_rows) & (slot < (tile + 1) * tile_rows)
            seen = jnp.where(inside, (mask_ref[b, tile] > 0).astype(jnp.float32), seen)
        visible = seen > 0.0
        rows = pl.ds(b * QBLK, QBLK)
        for g in range(groups):
            key_rows = kv_ref[:, g * 2 * HDIM:g * 2 * HDIM + HDIM]
            value_rows = kv_ref[:, g * 2 * HDIM + HDIM:(g + 1) * 2 * HDIM]
            for h in range(per_group):
                cols = pl.ds((g * per_group + h) * HDIM, HDIM)
                scores = lax.dot_general(
                    q_ref[rows, cols], key_rows, (((1,), (1,)), ((), ())),
                    preferred_element_type=jnp.float32) * scale
                masked = jnp.where(visible, scores, -1e30)
                top = jnp.max(masked, axis=1, keepdims=True)
                weights = jnp.where(visible, jnp.exp(masked - top), 0.0)
                total = jnp.sum(weights, axis=1, keepdims=True)
                total = jnp.where(total > 0.0, total, 1.0)
                probs = (weights / total).astype(jnp.bfloat16)
                o_ref[rows, cols] = jnp.dot(
                    probs, value_rows, preferred_element_type=jnp.float32).astype(jnp.bfloat16)


def attend(queries, kv_slots, block_mask):
    tokens, width = queries.shape
    return pl.pallas_call(
        attend_kernel,
        out_shape=jax.ShapeDtypeStruct((tokens, width), jnp.bfloat16),
        in_specs=[
            pl.BlockSpec(memory_space=pltpu.SMEM),
            pl.BlockSpec(memory_space=pltpu.VMEM),
            pl.BlockSpec(memory_space=pltpu.VMEM),
        ],
        out_specs=pl.BlockSpec(memory_space=pltpu.VMEM),
        cost_estimate=pl.CostEstimate(
            flops=4 * tokens * kv_slots.shape[0] * width, bytes_accessed=4 * tokens * width,
            transcendentals=tokens * kv_slots.shape[0] * width // HDIM),
        compiler_params=pltpu.CompilerParams(vmem_limit_bytes=24 * 1024 * 1024),
    )(block_mask, queries, kv_slots)


def local(
    image_rows,
    norm_gain,
    expand_weight,
    shrink_weight,
    projector,
    kv_weight,
    queries,
    send_list,
    block_mask,
):
    wanted = send_list[0]
    fold_part = jnp.dot(projector, kv_weight, preferred_element_type=jnp.float32).astype(jnp.bfloat16)
    fold_rows = lax.psum_scatter(fold_part, "tp", scatter_dimension=0, tiled=True)
    fold_rows = lax.all_gather(fold_rows, "seq", axis=1, tiled=True)
    normed = layer_norm(image_rows, norm_gain)
    hidden = jax.nn.gelu(
        jnp.dot(normed, expand_weight, preferred_element_type=jnp.float32), approximate=False
    ).astype(jnp.bfloat16)
    partial_value = jnp.dot(hidden, shrink_weight, preferred_element_type=jnp.float32).astype(jnp.bfloat16)
    own_sum = lax.psum_scatter(partial_value, "tp", scatter_dimension=1, tiled=True)
    share_width = own_sum.shape[1]
    own_rows = lax.dynamic_slice_in_dim(
        image_rows, lax.axis_index("tp") * share_width, share_width, 1
    )
    own_share = (own_rows.astype(jnp.float32) + own_sum.astype(jnp.float32)).astype(jnp.bfloat16)
    vit_out = lax.all_gather(own_share, "tp", axis=1, tiled=True)
    states = jnp.dot(vit_out, projector, preferred_element_type=jnp.float32).astype(jnp.bfloat16)
    outgoing = select_rows(own_share, wanted)
    arrived = lax.all_to_all(outgoing, "seq", split_axis=0, concat_axis=0, tiled=True)
    slot_rows = arrived.reshape(-1, share_width)
    kv_part = jnp.dot(slot_rows, fold_rows, preferred_element_type=jnp.float32).astype(jnp.bfloat16)
    kv_slots = lax.psum_scatter(kv_part, "tp", scatter_dimension=1, tiled=True)
    return (states, attend(queries, kv_slots, block_mask))


def solution(mesh):
    placed = (
        P("seq", None),
        P(),
        P(None, "tp"),
        P("tp", None),
        P(None, "tp"),
        P("tp", "seq"),
        P("seq", "tp"),
        P("seq", None, None),
        P("seq", None),
    )
    return jax.shard_map(
        local,
        mesh=mesh,
        in_specs=placed,
        out_specs=(P("seq", "tp"), P("seq", "tp")),
        check_vma=False,
    )
```

profile of v0, /device:TPU:0, one launch (start us, length us, event | category | flops | bytes accessed | tf_op | source)
XLA Modules:
  0.0 145.8 jit_solution(5948946665175045105)
XLA Ops:
  7.2 0.0 copy-start
  7.2 0.0 copy-start.5
  7.2 0.0 reduce-scatter.6.cloned.1.call-start
  7.2 5.3 %convolution_convert_fusion.1 = bf16[1280,256]{1,0:T(8,128)(2,1)} fusion(bf16[1280,2048]{1,0:T(8,128)(2,1)} %param.13, bf16[2048,256]{1,0:T(8,128)(2,1)} %param.14), kind=kOutput, calls=%fused_computation.1 | convolution fusion | flops 1342504960 | bytes 6946816 | tf_op jit(solution)/shard_map/dot_general | solution.py:93
  12.5 0.0 reduce-scatter.6.cloned.1.call-update
  12.6 0.0 reduce-scatter.4.cloned.1.call-start
  12.6 1.1 convert_reduce_fusion
  13.7 1.2 fusion.2
  14.9 0.0 copy-done
  14.9 0.0 copy-done.5
  14.9 0.0 copy-start.4
  15.0 5.7 %convolution_convert_fusion.3 = bf16[128,1280]{0,1:T(8,128)(2,1)} fusion(bf16[1280,1280]{1,0:T(8,128)(2,1)S(1)} %copy-done, bf16[1280,1280]{1,0:T(8,128)(2,1)} %param.11, bf16[128,1280]{1,0:T(8,128)(2,1)} %param.9, f32[1280]{0:T(1024)S(1)} %copy-done.5, f32[128]{0:T(128)S(1)} %add_rsqrt_fusion, f32[128]{0:T(128)S(1)} %broadcast_multiply_fusion), kind=kOutput, calls=%fused_computation.3 | convolution fusion | flops 850493440 | bytes 7215104 | tf_op jit(solution)/shard_map/dot_general | solution.py:100
  20.7 0.0 reduce-scatter.4.cloned.1.call-update
  20.7 0.0 all-gather.2.cloned.1.call-start
  20.7 17.1 %reduce-scatter.6.cloned.1.call-done = bf16[320,256]{1,0:T(8,128)(2,1)} async-done(((bf16[1280,256]{1,0:T(8,128)(2,1)}), bf16[320,256]{1,0:T(8,128)(2,1)}) %reduce-scatter.6.cloned.1.call-update) | async-done | bytes 163856 | tf_op jit(solution)/shard_map/reduce_scatter | solution.py:94
  37.9 0.0 all-gather.2.cloned.1.call-update
  37.9 0.0 reduce-scatter.8.cloned.1.call-start
  37.9 1.0 constant_dynamic-slice_fusion
  39.0 0.1 copy.14
  39.1 0.0 copy-done.4
  39.1 0.1 eq.15
  39.2 22.3 %reduce-scatter.4.cloned.1.call-done = bf16[128,320]{0,1:T(8,128)(2,1)} async-done(((bf16[128,1280]{0,1:T(8,128)(2,1)}), bf16[128,320]{0,1:T(8,128)(2,1)}) %reduce-scatter.4.cloned.1.call-update) | async-done | bytes 81936 | tf_op jit(solution)/shard_map/reduce_scatter | solution.py:101
  61.4 0.9 add_convert_fusion
  62.3 0.3 convolution_convert_fusion.4
  62.6 0.8 copy.13
  63.4 14.5 %all_to_all.5 = bf16[8,32,320]{2,1,0:T(8,128)(2,1)S(1)} all-to-all(bf16[8,32,320]{2,1,0:T(8,128)(2,1)} %bitcast.12), channel_id=1, replica_groups=mesh['seq'=8,'tp'=4] {'seq'}, dimensions={0} | all-to-all | bytes 327680 | tf_op jit(solution)/shard_map/all_to_all | solution.py:110
  77.9 28.5 %all-gather.2.cloned.1.call-done = bf16[320,2048]{1,0:T(8,128)(2,1)} async-done(((bf16[320,256]{1,0:T(8,128)(2,1)}), bf16[320,2048]{1,0:T(8,128)(2,1)}) %all-gather.2.cloned.1.call-update) | async-done | bytes 1310736 | tf_op jit(solution)/shard_map/all_gather | solution.py:95
  106.4 3.0 %convolution_convert_fusion = bf16[256,2048]{1,0:T(8,128)(2,1)} fusion(bf16[256,320]{1,0:T(8,128)(2,1)S(1)} %bitcast.11, bf16[320,2048]{1,0:T(8,128)(2,1)} %all-gather.2.cloned.1.call-done), kind=kOutput, calls=%fused_computation | convolution fusion | flops 336068608 | bytes 2523136 | tf_op jit(solution)/shard_map/dot_general | solution.py:112
  109.4 0.0 reduce-scatter.8.cloned.1.call-update
  109.4 0.0 copy-start.3
  109.4 6.1 %all_gather.6 = bf16[128,1280]{0,1:T(8,128)(2,1)S(1)} all-gather(bf16[128,320]{0,1:T(8,128)(2,1)S(1)} %add_convert_fusion), channel_id=1, replica_groups=mesh['seq'=8,'tp'=4] {'tp'}, dimensions={1}, use_global_device_ids=true | all-gather | bytes 409600 | tf_op jit(solution)/shard_map/all_gather | solution.py:107
  115.5 4.3 %convolution_convert_fusion.2 = bf16[128,2048]{1,0:T(8,128)(2,1)} fusion(bf16[128,1280]{0,1:T(8,128)(2,1)S(1)} %all_gather.6, bf16[1280,2048]{1,0:T(8,128)(2,1)} %param.13), kind=kOutput, calls=%fused_computation.2 | convolution fusion | flops 671350784 | bytes 6094848 | tf_op jit(solution)/shard_map/dot_general | solution.py:108
  119.8 13.3 %reduce-scatter.8.cloned.1.call-done.kv_ref = bf16[256,512]{1,0:T(8,128)(2,1)} async-done(((bf16[256,2048]{1,0:T(8,128)(2,1)}), bf16[256,512]{1,0:T(8,128)(2,1)}) %reduce-scatter.8.cloned.1.call-update) | async-done | bytes 262160 | tf_op jit(solution)/shard_map/reduce_scatter | solution.py:113
  133.1 0.0 copy-done.3
  133.1 0.0 copy-start.1
  133.1 1.2 copy-done.1
  134.3 0.0 copy-start.2
  134.3 0.9 copy-done.2
  135.3 4.0 %shard_map.104 = bf16[256,2048]{1,0:T(8,128)(2,1)} custom-call(s32[2,4]{1,0:T(2,128)S(1)} %copy-done.3, bf16[256,2048]{1,0:T(8,128)(2,1)S(1)} %copy-done.1, bf16[256,512]{1,0:T(8,128)(2,1)S(1)} %copy-done.2), custom_call_target="tpu_custom_call" | custom-call | flops 536870912 | bytes 2097152 | tf_op jit(solution)/shard_map/pallas_call | solution.py:65
  (2 shorter events, 0.0 us)
Async XLA Ops:
  7.2 7.8 %copy-start = (bf16[1280,1280]{1,0:T(8,128)(2,1)S(1)}, bf16[1280,1280]{1,0:T(8,128)(2,1)}, u32[]{:S(2)}) copy-start(bf16[1280,1280]{1,0:T(8,128)(2,1)} %param.12) | copy-start | bytes 9830404
  7.2 7.8 %copy-start.5 = (f32[1280]{0:T(1024)S(1)}, f32[1280]{0:T(1024)}, u32[]{:S(2)}) copy-start(f32[1280]{0:T(1024)} %param.10) | copy-start | bytes 15364
  7.2 30.7 %reduce-scatter.6.cloned.1.call-start = ((), (), s32[]{:S(2)}) async-start(), calls=%async_computation.5 | async-start | bytes 819200 | tf_op jit(solution)/shard_map/reduce_scatter | solution.py:94
  12.6 48.9 %reduce-scatter.4.cloned.1.call-start = ((), (), s32[]{:S(2)}) async-start(), calls=%async_computation.4 | async-start | bytes 409600 | tf_op jit(solution)/shard_map/reduce_scatter | solution.py:101
  14.9 24.1 %copy-start.4 = (s32[1,8,32]{2,1,0:T(8,128)S(1)}, s32[1,8,32]{2,1,0:T(8,128)}, u32[]{:S(2)}) copy-start(s32[1,8,32]{2,1,0:T(8,128)} %param.16) | copy-start | bytes 3076
  20.7 85.7 %all-gather.2.cloned.1.call-start = ((), (), s32[]{:S(2)}) async-start(), calls=%async_computation.6 | async-start | bytes 1474560 | tf_op jit(solution)/shard_map/all_gather | solution.py:95
  37.9 95.2 %reduce-scatter.8.cloned.1.call-start = ((), (), s32[]{:S(2)}) async-start(), calls=%async_computation.7 | async-start | bytes 1310720 | tf_op jit(solution)/shard_map/reduce_scatter | solution.py:113
  109.4 23.7 %copy-start.3 = (s32[2,4]{1,0:T(2,128)S(1)}, s32[2,4]{1,0:T(2,128)}, u32[]{:S(2)}) copy-start(s32[2,4]{1,0:T(2,128)} %mask_ref.1) | copy-start | bytes 100
  133.1 1.2 copy-start.1
  134.3 0.9 copy-start.2
Sparse Core Ops, SparseCore 0:
  12.7 25.1 reduce-scatter.5
  40.9 20.4 reduce-scatter.3
  63.7 42.6 all-gather.1
  109.5 23.5 reduce-scatter.7
where the time goes:
time: 146 us
  waiting for transfers between devices  81.3 us (56%)
  blocking collectives  20.5 us (14%)
  matrix products  18.6 us (13%)
  between operations  13.8 us (9%)
  local copies, waits for them, and re-layouts  4.22 us (3%)
  Pallas kernels  3.97 us (3%)
  other arithmetic  3.23 us (2%)
    all_gather x1, waiting for transfers between devices, local(): fold_rows = lax.all_gather(fold_rows, 'seq', axis=1, tiled=True)  28.5 us
    reduce_scatter x1, waiting for transfers between devices, local(): lax.psum_scatter(partial_value, 'tp', scatter_dimension=1, tiled=True)  22.3 us
    reduce_scatter x1, waiting for transfers between devices, local(): lax.psum_scatter(fold_part, 'tp', scatter_dimension=0, tiled=True)  17.1 us
    all_to_all x1, blocking collectives, local(): lax.all_to_all(outgoing, 'seq', split_axis=0, concat_axis=0, tiled=True)  14.5 us
    reduce_scatter x1, waiting for transfers between devices, local(): kv_slots = lax.psum_scatter(kv_part, 'tp', scatter_dimension=1, tiled=True)  13.3 us
    all_gather x1, blocking collectives, local(): vit_out = lax.all_gather(own_share, 'tp', axis=1, tiled=True)  6.06 us
    dot_general x1, matrix products, local(): jnp.dot(hidden, shrink_weight, preferred_element_type=jnp.float32)  5.7 us
    dot_general x1, matrix products, local(): jnp.dot(projector, kv_weight, preferred_element_type=jnp.float32)  5.3 us
  transfers between devices with their start and end apart: 4, of which 4 were waited for; matrix products, arithmetic and copies ran while one was open for 11% of the time, Pallas kernels for 0%

commit v1 on v0

--- a/solution.py
+++ b/solution.py
@@ -1,3 +1,4 @@
+import functools
 import math
 
 import jax
@@ -78,6 +79,232 @@
     )(block_mask, queries, kv_slots)
 
 
+MESH = pl.DeviceIdType.MESH
+
+
+def exchange_kernel(n_seq, n_tp, image_ref, gain_ref, expand_ref, shrink_ref, proj_ref, kvw_ref, hot_ref,
+                    vit_ref, kv_ref,
+                    fold_out, fold_in, gathered, mine, parts, parts_in, image_cut, chosen, slots,
+                    a_s, a_r, b_s, b_r, g_r, up_s, down_s, y_s, x_s, m_r, v_s, v_r, s_s, s_r, f_s, f_r):
+    s = lax.axis_index("seq")
+    t = lax.axis_index("tp")
+    z, y = s // 2, s % 2
+    depth = proj_ref.shape[0] // n_tp
+    cap = hot_ref.shape[0] // n_seq
+
+    barrier = pltpu.get_barrier_semaphore()
+    for j in range(1, n_tp):
+        pl.semaphore_signal(barrier, inc=1, device_id=(s, lax.rem(t + j, n_tp)), device_id_type=MESH)
+    for j in range(1, n_seq):
+        pl.semaphore_signal(barrier, inc=1, device_id=(lax.rem(s + j, n_seq), t), device_id_type=MESH)
+
+    def remote(src, dst, send, recv, where):
+        return pltpu.make_async_remote_copy(src_ref=src, dst_ref=dst, send_sem=send, recv_sem=recv,
+                                            device_id=where, device_id_type=MESH)
+
+    sent = []
+
+    def go(copy):
+        copy.start()
+        sent.append(copy)
+
+    def fold_quarter(q):
+        rows = pl.ds(pl.multiple_of(q * depth, 64), depth)
+        return jnp.dot(proj_ref[rows, :], kvw_ref[...], preferred_element_type=jnp.float32)
+
+    for j in range(1, n_tp):
+        peer = lax.rem(t + j, n_tp)
+        fold_out[j] = fold_quarter(peer).astype(jnp.bfloat16)
+        if j == 1:
+            pl.semaphore_wait(barrier, n_tp + n_seq - 2)
+        go(remote(fold_out.at[j], fold_in.at[j], a_s.at[j], a_r.at[j], (s, peer)))
+    own_fold = fold_quarter(t)
+
+    values = image_ref[...].astype(jnp.float32)
+    center = values - jnp.mean(values, axis=1, keepdims=True)
+    spread = jnp.mean(center * center, axis=1, keepdims=True)
+    normed = (center * lax.rsqrt(spread + 1e-05) * gain_ref[...]).astype(jnp.bfloat16)
+    wide = jnp.dot(normed, expand_ref[...], preferred_element_type=jnp.float32)
+    hidden = (0.5 * wide * (1.0 + lax.erf(wide * math.sqrt(0.5)))).astype(jnp.bfloat16)
+    partial = jnp.dot(hidden, shrink_ref[...], preferred_element_type=jnp.float32)
+    for q in range(n_tp):
+        parts[q] = partial[:, q * depth:(q + 1) * depth].astype(jnp.bfloat16)
+        image_cut[q] = values[:, q * depth:(q + 1) * depth]
+    for j in range(1, n_tp):
+        peer = lax.rem(t + j, n_tp)
+        go(remote(parts.at[peer], parts_in.at[j], b_s.at[j], b_r.at[j], (s, peer)))
+
+    def arrive(buf, sem):
+        pltpu.make_async_copy(buf, buf, sem).wait()
+
+    for j in range(1, n_tp):
+        arrive(fold_in.at[j], a_r.at[j])
+        own_fold += fold_in[j].astype(jnp.float32)
+    gathered[s] = own_fold.astype(jnp.bfloat16)
+
+    def up(zz):
+        i = 2 * zz + y
+        return remote(gathered.at[i], gathered.at[i], up_s.at[zz], g_r.at[i], (s + 2, t))
+
+    def down(zz):
+        i = 2 * zz + y
+        return remote(gathered.at[i], gathered.at[i], down_s.at[zz], g_r.at[i], (s - 2, t))
+
+    def across(zz):
+        i = 2 * zz + y
+        return remote(gathered.at[i], gathered.at[i], y_s.at[zz], g_r.at[i], (2 * z + 1 - y, t))
+
+    def deliver(zz, yy):
+        i = 2 * zz + yy
+        return remote(gathered.at[i], mine.at[2 * t + yy], x_s.at[i], m_r.at[2 * t + yy], (s, zz))
+
+    def hand_on(zz, yy):
+        @pl.when(zz != t)
+        def _():
+            deliver(zz, yy).start()
+
+        @pl.when(zz == t)
+        def _():
+            mine[2 * t + yy] = gathered[2 * zz + yy]
+
+    @pl.when(z < n_tp - 1)
+    def _():
+        up(z).start()
+
+    @pl.when(z > 0)
+    def _():
+        down(z).start()
+
+    across(z).start()
+    hand_on(z, y)
+
+    share = parts[t].astype(jnp.float32)
+    for j in range(1, n_tp):
+        arrive(parts_in.at[j], b_r.at[j])
+        share += parts_in[j].astype(jnp.float32)
+    share = (image_cut[t] + share).astype(jnp.bfloat16)
+    vit_ref[t] = share
+    picked = jnp.dot(hot_ref[...], share, preferred_element_type=jnp.float32).astype(jnp.bfloat16)
+    chosen[...] = picked.reshape(n_seq, cap, depth)
+    slots[t, s] = chosen[s]
+    for j in range(1, n_seq):
+        peer = lax.rem(s + j, n_seq)
+        go(remote(chosen.at[peer], slots.at[t, s], s_s.at[j], s_r.at[s], (peer, t)))
+    for j in range(1, n_tp):
+        go(remote(vit_ref.at[t], vit_ref.at[t], v_s.at[j], v_r.at[t], (s, lax.rem(t + j, n_tp))))
+
+    def z_step(k):
+        @pl.when(z - k >= 0)
+        def _():
+            arrive(gathered.at[2 * (z - k) + y], g_r.at[2 * (z - k) + y])
+
+            @pl.when(z < n_tp - 1)
+            def _():
+                up(z - k).start()
+            across(z - k).start()
+            hand_on(z - k, y)
+
+        @pl.when(z + k < n_tp)
+        def _():
+            arrive(gathered.at[2 * (z + k) + y], g_r.at[2 * (z + k) + y])
+
+            @pl.when(z > 0)
+            def _():
+                down(z + k).start()
+            across(z + k).start()
+            hand_on(z + k, y)
+
+    def y_step(zz):
+        arrive(gathered.at[2 * zz + 1 - y], g_r.at[2 * zz + 1 - y])
+        hand_on(zz, 1 - y)
+
+    for j in range(1, n_seq):
+        peer = lax.rem(s + j, n_seq)
+        arrive(slots.at[t, peer], s_r.at[peer])
+    for j in range(1, n_tp):
+        go(remote(slots.at[t], slots.at[t], f_s.at[j], f_r.at[t], (s, lax.rem(t + j, n_tp))))
+    z_step(1)
+    y_step(z)
+    for k in range(1, n_tp):
+        if k > 1:
+            z_step(k)
+
+        @pl.when(z - k >= 0)
+        def _():
+            y_step(z - k)
+
+        @pl.when(z + k < n_tp)
+        def _():
+            y_step(z + k)
+
+    for j in range(1, n_tp):
+        peer = lax.rem(t + j, n_tp)
+        arrive(slots.at[peer], f_r.at[peer])
+        arrive(vit_ref.at[peer], v_r.at[peer])
+    for j in range(1, n_tp):
+        peer = lax.rem(t + j, n_tp)
+        for yy in range(2):
+            arrive(mine.at[2 * peer + yy], m_r.at[2 * peer + yy])
+    width = kvw_ref.shape[1]
+    for yy in range(2):
+        total = None
+        for q in range(n_tp):
+            term = jnp.dot(slots[q].reshape(n_seq * cap, depth), mine[2 * q + yy], preferred_element_type=jnp.float32)
+            total = term if total is None else total + term
+        kv_ref[:, yy * width:(yy + 1) * width] = total.astype(jnp.bfloat16)
+
+    for copy in sent:
+        copy.wait_send()
+    for zz in range(n_tp):
+        across(zz).wait_send()
+
+        @pl.when((z < n_tp - 1) & (zz <= z))
+        def _():
+            up(zz).wait_send()
+
+        @pl.when((z > 0) & (zz >= z))
+        def _():
+            down(zz).wait_send()
+
+        @pl.when(zz != t)
+        def _():
+            for yy in range(2):
+                deliver(zz, yy).wait_send()
+
+
+def exchange(n_seq, n_tp, image_rows, norm_gain, expand_weight, shrink_weight, projector, kv_weight, hot):
+    rows, features = image_rows.shape
+    depth = features // n_tp
+    width = kv_weight.shape[1]
+    cap = hot.shape[0] // n_seq
+    bf16, f32 = jnp.bfloat16, jnp.float32
+    dma = pltpu.SemaphoreType.DMA
+    vmem = pl.BlockSpec(memory_space=pltpu.VMEM)
+    return pl.pallas_call(
+        functools.partial(exchange_kernel, n_seq, n_tp),
+        out_shape=(jax.ShapeDtypeStruct((n_tp, rows, depth), bf16),
+                   jax.ShapeDtypeStruct((hot.shape[0], 2 * width), bf16)),
+        in_specs=[vmem] * 7,
+        out_specs=(vmem, vmem),
+        scratch_shapes=[
+            pltpu.VMEM((n_tp, depth, width), bf16),
+            pltpu.VMEM((n_tp, depth, width), bf16),
+            pltpu.VMEM((n_seq, depth, width), bf16),
+            pltpu.VMEM((2 * n_tp, depth, width), bf16),
+            pltpu.VMEM((n_tp, rows, depth), bf16),
+            pltpu.VMEM((n_tp, rows, depth), bf16),
+            pltpu.VMEM((n_tp, rows, depth), f32),
+            pltpu.VMEM((n_seq, cap, depth), bf16),
+            pltpu.VMEM((n_tp, n_seq, cap, depth), bf16),
+            dma((n_tp,)), dma((n_tp,)), dma((n_tp,)), dma((n_tp,)),
+            dma((n_seq,)), dma((n_tp,)), dma((n_tp,)), dma((n_tp,)), dma((n_seq,)), dma((2 * n_tp,)),
+            dma((n_tp,)), dma((n_tp,)), dma((n_seq,)), dma((n_seq,)), dma((n_tp,)), dma((n_tp,)),
+        ],
+        compiler_params=pltpu.CompilerParams(
+            collective_id=0, has_side_effects=True, vmem_limit_bytes=48 * 1024 * 1024),
+    )(image_rows, norm_gain.reshape(1, -1), expand_weight, shrink_weight, projector, kv_weight, hot)
+
+
 def local(
     image_rows,
     norm_gain,
@@ -90,6 +317,15 @@
     block_mask,
 ):
     wanted = send_list[0]
+    n_seq, n_tp = lax.axis_size("seq"), lax.axis_size("tp")
+    if n_seq == 2 * n_tp and kv_weight.shape[1] == 2 * HDIM and wanted.shape[1] % 16 == 0:
+        flat = wanted.reshape(-1)
+        hot = (flat[:, None] == jnp.arange(image_rows.shape[0], dtype=jnp.int32)[None, :]).astype(jnp.bfloat16)
+        shares, kv_slots = exchange(
+            n_seq, n_tp, image_rows, norm_gain, expand_weight, shrink_weight, projector, kv_weight, hot)
+        vit_out = jnp.transpose(shares, (1, 0, 2)).reshape(image_rows.shape)
+        states = jnp.dot(vit_out, projector, preferred_element_type=jnp.float32).astype(jnp.bfloat16)
+        return (states, attend(queries, kv_slots, block_mask))
     fold_part = jnp.dot(projector, kv_weight, preferred_element_type=jnp.float32).astype(jnp.bfloat16)
     fold_rows = lax.psum_scatter(fold_part, "tp", scatter_dimension=0, tiled=True)
     fold_rows = lax.all_gather(fold_rows, "seq", axis=1, tiled=True)

time: 146 us -> 66.7 us (0.46)
  the two profiles are of different devices: /device:TPU:0 before, /device:TPU:3 now
where the time goes in v1:
time: 66.7 us; the launch traced here: 66 us
  Pallas kernels  55.1 us (83%)
  local copies, waits for them, and re-layouts  5.84 us (9%)
  matrix products  4.22 us (6%)
  between operations  0.68 us (1%)
    pallas_call x1, Pallas kernels, exchange(): pl.pallas_call(functools.partial(exchange_kernel, n_seq, n_tp), out_shape...  51.2 us
    dot_general x1, matrix products, local(): jnp.dot(vit_out, projector, preferred_element_type=jnp.float32)  4.22 us
    unnamed x10, local copies, waits for them, and re-layouts  4.13 us
    pallas_call x1, Pallas kernels, attend(): pl.pallas_call(attend_kernel, out_shape=jax.ShapeDtypeStruct((tokens, wid...  3.97 us

profile of v1, /device:TPU:3, one launch (start us, length us, event | category | flops | bytes accessed | tf_op | source)
XLA Modules:
  0.0 66.0 jit_solution(10053207901176042579)
XLA Ops:
  0.6 0.8 %eq.15 = s32[256]{0:T(256)S(1)} reshape(s32[1,8,32]{2,1,0:T(8,128)} %param.16) | data formatting | bytes 2048 | tf_op jit(solution)/shard_map/eq | solution.py:323
  1.4 0.7 %reshape.11.gain_ref = f32[1,1280]{1,0:T(1,128)S(1)} reshape(f32[1280]{0:T(1024)} %param.10) | data formatting | bytes 10240 | tf_op jit(solution)/shard_map/reshape | solution.py:305
  2.1 0.1 fusion.hot_ref
  2.2 0.0 copy-start
  2.2 1.9 %copy-done = bf16[1280,1280]{1,0:T(8,128)(2,1)S(1)} copy-done((bf16[1280,1280]{1,0:T(8,128)(2,1)S(1)}, bf16[1280,1280]{1,0:T(8,128)(2,1)}, u32[]{:S(2)}) %copy-start) | copy-done | bytes 3276824
  4.1 0.0 copy-start.1
  4.1 1.2 %copy-done.1 = bf16[2048,256]{1,0:T(8,128)(2,1)S(1)} copy-done((bf16[2048,256]{1,0:T(8,128)(2,1)S(1)}, bf16[2048,256]{1,0:T(8,128)(2,1)}, u32[]{:S(2)}) %copy-start.1) | copy-done | bytes 1048600
  5.4 0.0 copy-start.3
  5.4 1.0 %copy-done.3 = bf16[128,1280]{1,0:T(8,128)(2,1)S(1)} copy-done((bf16[128,1280]{1,0:T(8,128)(2,1)S(1)}, bf16[128,1280]{1,0:T(8,128)(2,1)}, u32[]{:S(2)}) %copy-start.3) | copy-done | bytes 327704
  6.3 51.2 %shard_map.104 = (bf16[4,128,320]{2,1,0:T(8,128)(2,1)S(1)}, bf16[256,512]{1,0:T(8,128)(2,1)S(1)}) custom-call(bf16[128,1280]{1,0:T(8,128)(2,1)S(1)} %copy-done.3, f32[1,1280]{1,0:T(1,128)S(1)} %reshape.11.gain_ref, bf16[1280,1280]{1,0:T(8,128)(2,1)S(1)} %copy-done, bf16[1280,1280]{1,0:T(8,128)(2,1)} %shrink_ref.1, bf16[1280,2048]{1,0:T(8,128)(2,1)} %proj_ref.1, ...), custom_call_target="tpu_custom_call" | custom-call | tf_op jit(solution)/shard_map/pallas_call | solution.py:283
  57.5 0.0 copy-start.2
  57.5 0.0 copy-start.4
  57.5 0.2 copy.11
  57.8 4.2 %convolution_convert_fusion = bf16[128,2048]{1,0:T(8,128)(2,1)} fusion(bf16[128,1280]{0,1:T(8,128)(2,1)S(1)} %bitcast.5, bf16[1280,2048]{1,0:T(8,128)(2,1)} %proj_ref.1), kind=kOutput, calls=%fused_computation | convolution fusion | flops 671350784 | bytes 6094848 | tf_op jit(solution)/shard_map/dot_general | solution.py:327
  62.0 0.0 copy-done.2
  62.0 0.0 copy-done.4
  62.0 4.0 %shard_map.105 = bf16[256,2048]{1,0:T(8,128)(2,1)} custom-call(s32[2,4]{1,0:T(2,128)S(1)} %copy-done.4, bf16[256,2048]{1,0:T(8,128)(2,1)S(1)} %copy-done.2, bf16[256,512]{1,0:T(8,128)(2,1)S(1)} %get-tuple-element.5.kv_ref), custom_call_target="tpu_custom_call" | custom-call | flops 536870912 | bytes 2097152 | tf_op jit(solution)/shard_map/pallas_call | solution.py:66
Async XLA Ops:
  2.2 1.9 %copy-start = (bf16[1280,1280]{1,0:T(8,128)(2,1)S(1)}, bf16[1280,1280]{1,0:T(8,128)(2,1)}, u32[]{:S(2)}) copy-start(bf16[1280,1280]{1,0:T(8,128)(2,1)} %expand_ref.1) | copy-start | bytes 9830404
  4.1 1.2 %copy-start.1 = (bf16[2048,256]{1,0:T(8,128)(2,1)S(1)}, bf16[2048,256]{1,0:T(8,128)(2,1)}, u32[]{:S(2)}) copy-start(bf16[2048,256]{1,0:T(8,128)(2,1)} %kvw_ref.1) | copy-start | bytes 3145732
  5.4 1.0 %copy-start.3 = (bf16[128,1280]{1,0:T(8,128)(2,1)S(1)}, bf16[128,1280]{1,0:T(8,128)(2,1)}, u32[]{:S(2)}) copy-start(bf16[128,1280]{1,0:T(8,128)(2,1)} %image_ref.1) | copy-start | bytes 983044
  57.5 4.5 %copy-start.2 = (bf16[256,2048]{1,0:T(8,128)(2,1)S(1)}, bf16[256,2048]{1,0:T(8,128)(2,1)}, u32[]{:S(2)}) copy-start(bf16[256,2048]{1,0:T(8,128)(2,1)} %q_ref.1) | copy-start | bytes 3145732
  57.5 4.5 %copy-start.4 = (s32[2,4]{1,0:T(2,128)S(1)}, s32[2,4]{1,0:T(2,128)}, u32[]{:S(2)}) copy-start(s32[2,4]{1,0:T(2,128)} %mask_ref.1) | copy-start | bytes 100

commit v2 on v0

--- a/solution.py
+++ b/solution.py
@@ -1,3 +1,4 @@
+import functools
 import math
 
 import jax
@@ -78,6 +79,285 @@
     )(block_mask, queries, kv_slots)
 
 
+MESH = pl.DeviceIdType.MESH
+
+
+def exchange_kernel(n_seq, n_tp, image_ref, gain_ref, want_ref, expand_any, shrink_any, proj_any, kvw_any,
+                    states_ref, kv_ref,
+                    expand_ref, shrink_ref, proj_ref, kvw_ref,
+                    pair_out, pair_in, cross_out, cross_in, gathered, other, parts, parts_in, image_cut,
+                    shares, chosen, slots,
+                    l_s, a_s, a_r, c_s, c_r, b_s, b_r, g_r, up_s, down_s, y_s, x_s, m_r, v_s, v_r, s_s, s_r, f_s, f_r):
+    s = lax.axis_index("seq")
+    t = lax.axis_index("tp")
+    z, y = s // 2, s % 2
+    x, c = t // 2, t % 2
+    last = n_tp - 1
+    core, over, skew = 2 * x + 1 - c, 2 * (1 - x) + c, 2 * (1 - x) + 1 - c
+    depth = proj_ref.shape[0] // n_tp
+    half = 2 * depth
+    cap = want_ref.shape[2]
+
+    barrier = pltpu.get_barrier_semaphore()
+    for j in range(1, n_tp):
+        pl.semaphore_signal(barrier, inc=1, device_id=(s, lax.rem(t + j, n_tp)), device_id_type=MESH)
+    for j in range(1, n_seq):
+        pl.semaphore_signal(barrier, inc=1, device_id=(lax.rem(s + j, n_seq), t), device_id_type=MESH)
+
+    def half_rows(h):
+        return pl.ds(pl.multiple_of(h * half, 128), half)
+
+    loads = [
+        pltpu.make_async_copy(kvw_any, kvw_ref, l_s.at[0]),
+        pltpu.make_async_copy(proj_any.at[half_rows(1 - c)], proj_ref.at[half_rows(1 - c)], l_s.at[1]),
+        pltpu.make_async_copy(proj_any.at[half_rows(c)], proj_ref.at[half_rows(c)], l_s.at[2]),
+        pltpu.make_async_copy(expand_any, expand_ref, l_s.at[3]),
+        pltpu.make_async_copy(shrink_any, shrink_ref, l_s.at[4]),
+    ]
+    for load in loads:
+        load.start()
+
+    def remote(src, dst, send, recv, where):
+        return pltpu.make_async_remote_copy(src_ref=src, dst_ref=dst, send_sem=send, recv_sem=recv,
+                                            device_id=where, device_id_type=MESH)
+
+    def arrive(buf, sem):
+        pltpu.make_async_copy(buf, buf, sem).wait()
+
+    sent = []
+
+    def go(copy):
+        copy.start()
+        sent.append(copy)
+
+    def fold_half(h):
+        return jnp.dot(proj_ref[half_rows(h), :], kvw_ref[...], preferred_element_type=jnp.float32)
+
+    loads[0].wait()
+    loads[1].wait()
+    pair_out[...] = fold_half(1 - c).astype(jnp.bfloat16)
+    pl.semaphore_wait(barrier, n_tp + n_seq - 2)
+    go(remote(pair_out, pair_in, a_s, a_r, (s, core)))
+    loads[2].wait()
+    own_fold = fold_half(c)
+    arrive(pair_in, a_r)
+    own_fold += pair_in[...].astype(jnp.float32)
+    cross_out[...] = own_fold.astype(jnp.bfloat16)
+    holds = z // 2 == x
+
+    def cross():
+        return remote(cross_out, cross_in, c_s, c_r, (s, over))
+
+    @pl.when(z // 2 != x)
+    def _():
+        cross().start()
+
+    values = image_ref[...].astype(jnp.float32)
+    center = values - jnp.mean(values, axis=1, keepdims=True)
+    spread = jnp.mean(center * center, axis=1, keepdims=True)
+    normed = (center * lax.rsqrt(spread + 1e-05) * gain_ref[...][None, :]).astype(jnp.bfloat16)
+    loads[3].wait()
+    wide = jnp.dot(normed, expand_ref[...], preferred_element_type=jnp.float32)
+    hidden = (0.5 * wide * (1.0 + lax.erf(wide * math.sqrt(0.5)))).astype(jnp.bfloat16)
+    loads[4].wait()
+    partial = jnp.dot(hidden, shrink_ref[...], preferred_element_type=jnp.float32)
+    for q in range(n_tp):
+        parts[q] = partial[:, q * depth:(q + 1) * depth].astype(jnp.bfloat16)
+        image_cut[q] = values[:, q * depth:(q + 1) * depth]
+    for j in range(1, n_tp):
+        peer = lax.rem(t + j, n_tp)
+        go(remote(parts.at[peer], parts_in.at[j], b_s.at[j], b_r.at[j], (s, peer)))
+
+    def place(zl, yy, ch):
+        return (zl * 2 + yy) * 2 + ch
+
+    def up(i):
+        return remote(gathered.at[i], gathered.at[i], up_s.at[i], g_r.at[i], (s + 2, t))
+
+    def down(i):
+        return remote(gathered.at[i], gathered.at[i], down_s.at[i], g_r.at[i], (s - 2, t))
+
+    def across(i):
+        return remote(gathered.at[i], gathered.at[i], y_s.at[i], g_r.at[i], (2 * z + 1 - y, t))
+
+    def hand(i, k):
+        return remote(gathered.at[i], other.at[k], x_s.at[i], m_r.at[k], (s, core))
+
+    def hand_on(zl, yy, ch):
+        @pl.when(zl != c)
+        def _():
+            hand(place(zl, yy, ch), 2 * yy + ch).start()
+
+    def relay(zl, ch):
+        i = place(zl, y, ch)
+        zz = 2 * x + zl
+
+        @pl.when(z != zz)
+        def _():
+            arrive(gathered.at[i], g_r.at[i])
+
+        @pl.when((z >= zz) & (z < last))
+        def _():
+            up(i).start()
+
+        @pl.when((z <= zz) & (z > 0))
+        def _():
+            down(i).start()
+
+        across(i).start()
+        hand_on(zl, y, ch)
+
+    def y_relay(zl, ch):
+        i = place(zl, 1 - y, ch)
+        arrive(gathered.at[i], g_r.at[i])
+        hand_on(zl, 1 - y, ch)
+
+    first = (z + 2 * (1 - x)) // last
+    second = 1 - first
+
+    @pl.when(holds)
+    def _():
+        arrive(cross_in, c_r)
+        for ch in range(2):
+            rows = slice(ch * depth, (ch + 1) * depth)
+            gathered[place(first, y, ch)] = (
+                cross_out[rows, :].astype(jnp.float32) + cross_in[rows, :].astype(jnp.float32)).astype(jnp.bfloat16)
+            relay(first, ch)
+
+    share = parts[t].astype(jnp.float32)
+    for j in range(1, n_tp):
+        arrive(parts_in.at[j], b_r.at[j])
+        share += parts_in[j].astype(jnp.float32)
+    share = (image_cut[t] + share).astype(jnp.bfloat16)
+    shares[t] = share
+    row_id = lax.broadcasted_iota(jnp.int32, (share.shape[0], cap), 0)
+    for d in range(n_seq):
+        hot = (row_id == want_ref[0, d:d + 1, :]).astype(jnp.float32).astype(jnp.bfloat16)
+        chosen[d] = lax.dot_general(
+            hot, share, (((0,), (0,)), ((), ())), preferred_element_type=jnp.float32).astype(jnp.bfloat16)
+    slots[t, s] = chosen[s]
+    for j in range(1, n_seq):
+        peer = lax.rem(s + j, n_seq)
+        go(remote(chosen.at[peer], slots.at[t, s], s_s.at[j], s_r.at[s], (peer, t)))
+    go(remote(shares.at[t], shares.at[t], v_s.at[1], v_r.at[t], (s, core)))
+    go(remote(shares.at[t], shares.at[t], v_s.at[2], v_r.at[t], (s, over)))
+
+    @pl.when(z // 2 != x)
+    def _():
+        for ch in range(2):
+            relay(first, ch)
+
+    for j in range(1, n_seq):
+        peer = lax.rem(s + j, n_seq)
+        arrive(slots.at[t, peer], s_r.at[peer])
+    go(remote(slots.at[t], slots.at[t], f_s.at[1], f_r.at[t], (s, core)))
+    go(remote(slots.at[t], slots.at[t], f_s.at[2], f_r.at[t], (s, over)))
+    arrive(shares.at[over], v_r.at[over])
+    go(remote(shares.at[over], shares.at[over], v_s.at[3], v_r.at[over], (s, core)))
+    relay(second, 0)
+    y_relay(first, 0)
+    relay(second, 1)
+    y_relay(first, 1)
+    arrive(slots.at[over], f_r.at[over])
+    go(remote(slots.at[over], slots.at[over], f_s.at[3], f_r.at[over], (s, core)))
+
+    arrive(shares.at[core], v_r.at[core])
+    arrive(shares.at[skew], v_r.at[skew])
+    n_cut = 4
+    cut = states_ref.shape[1] // n_cut
+    for n in range(n_cut):
+        cols = slice(n * cut, (n + 1) * cut)
+        total = None
+        for q in range(n_tp):
+            term = jnp.dot(shares[q], proj_ref[q * depth:(q + 1) * depth, cols], preferred_element_type=jnp.float32)
+            total = term if total is None else total + term
+        states_ref[:, cols] = total.astype(jnp.bfloat16)
+
+    arrive(slots.at[core], f_r.at[core])
+    arrive(slots.at[skew], f_r.at[skew])
+    for ch in range(2):
+        y_relay(second, ch)
+    width = kvw_ref.shape[1]
+    for yy in range(2):
+        total = None
+        for ch in range(2):
+            rows = slots[2 * c + ch].reshape(n_seq * cap, depth)
+            term = jnp.dot(rows, gathered[place(c, yy, ch)], preferred_element_type=jnp.float32)
+            total = term if total is None else total + term
+        for ch in range(2):
+            arrive(other.at[2 * yy + ch], m_r.at[2 * yy + ch])
+            rows = slots[2 * (1 - c) + ch].reshape(n_seq * cap, depth)
+            total += jnp.dot(rows, other[2 * yy + ch], preferred_element_type=jnp.float32)
+        kv_ref[:, yy * width:(yy + 1) * width] = total.astype(jnp.bfloat16)
+
+    for copy in sent:
+        copy.wait_send()
+
+    @pl.when(z // 2 != x)
+    def _():
+        cross().wait_send()
+
+    for zl in range(2):
+        zz = 2 * x + zl
+        for ch in range(2):
+            i = place(zl, y, ch)
+            across(i).wait_send()
+
+            @pl.when((z >= zz) & (z < last))
+            def _():
+                up(i).wait_send()
+
+            @pl.when((z <= zz) & (z > 0))
+            def _():
+                down(i).wait_send()
+
+            @pl.when(zl != c)
+            def _():
+                for yy in range(2):
+                    hand(place(zl, yy, ch), 2 * yy + ch).wait_send()
+
+
+def exchange(n_seq, n_tp, image_rows, norm_gain, send_list, expand_weight, shrink_weight, projector, kv_weight):
+    rows, features = image_rows.shape
+    depth = features // n_tp
+    width = kv_weight.shape[1]
+    cap = send_list.shape[2]
+    bf16, f32 = jnp.bfloat16, jnp.float32
+    dma = pltpu.SemaphoreType.DMA
+    vmem = pl.BlockSpec(memory_space=pltpu.VMEM)
+    anywhere = pl.BlockSpec(memory_space=pl.ANY)
+    return pl.pallas_call(
+        functools.partial(exchange_kernel, n_seq, n_tp),
+        out_shape=(jax.ShapeDtypeStruct((rows, projector.shape[1]), bf16),
+                   jax.ShapeDtypeStruct((n_seq * cap, 2 * width), bf16)),
+        in_specs=[vmem] * 3 + [anywhere] * 4,
+        out_specs=(vmem, vmem),
+        scratch_shapes=[
+            pltpu.VMEM(expand_weight.shape, bf16),
+            pltpu.VMEM(shrink_weight.shape, bf16),
+            pltpu.VMEM(projector.shape, bf16),
+            pltpu.VMEM(kv_weight.shape, bf16),
+            pltpu.VMEM((2 * depth, width), bf16),
+            pltpu.VMEM((2 * depth, width), bf16),
+            pltpu.VMEM((2 * depth, width), bf16),
+            pltpu.VMEM((2 * depth, width), bf16),
+            pltpu.VMEM((8, depth, width), bf16),
+            pltpu.VMEM((4, depth, width), bf16),
+            pltpu.VMEM((n_tp, rows, depth), bf16),
+            pltpu.VMEM((n_tp, rows, depth), bf16),
+            pltpu.VMEM((n_tp, rows, depth), f32),
+            pltpu.VMEM((n_tp, rows, depth), bf16),
+            pltpu.VMEM((n_seq, cap, depth), bf16),
+            pltpu.VMEM((n_tp, n_seq, cap, depth), bf16),
+            dma((5,)), dma, dma, dma, dma, dma((n_tp,)), dma((n_tp,)),
+            dma((8,)), dma((8,)), dma((8,)), dma((8,)), dma((8,)), dma((4,)),
+            dma((n_tp,)), dma((n_tp,)), dma((n_seq,)), dma((n_seq,)), dma((n_tp,)), dma((n_tp,)),
+        ],
+        compiler_params=pltpu.CompilerParams(
+            collective_id=0, has_side_effects=True, vmem_limit_bytes=56 * 1024 * 1024),
+    )(image_rows, norm_gain, send_list, expand_weight, shrink_weight, projector, kv_weight)
+
+
 def local(
     image_rows,
     norm_gain,
@@ -90,6 +370,11 @@
     block_mask,
 ):
     wanted = send_list[0]
+    n_seq, n_tp = lax.axis_size("seq"), lax.axis_size("tp")
+    if n_seq == 8 and n_tp == 4 and kv_weight.shape[1] == 2 * HDIM and wanted.shape[1] % 16 == 0:
+        states, kv_slots = exchange(
+            n_seq, n_tp, image_rows, norm_gain, send_list, expand_weight, shrink_weight, projector, kv_weight)
+        return (states, attend(queries, kv_slots, block_mask))
     fold_part = jnp.dot(projector, kv_weight, preferred_element_type=jnp.float32).astype(jnp.bfloat16)
     fold_rows = lax.psum_scatter(fold_part, "tp", scatter_dimension=0, tiled=True)
     fold_rows = lax.all_gather(fold_rows, "seq", axis=1, tiled=True)

time: 146 us -> 61.3 us (0.42)
  the two profiles are of different devices: /device:TPU:0 before, /device:TPU:3 now
where the time goes in v2:
time: 61.3 us; the launch traced here: 61.1 us
  Pallas kernels  57.6 us (94%)
  local copies, waits for them, and re-layouts  2.83 us (5%)
  between operations  0.68 us (1%)
    pallas_call x1, Pallas kernels, exchange(): pl.pallas_call(functools.partial(exchange_kernel, n_seq, n_tp), out_shape...  53.7 us
    pallas_call x1, Pallas kernels, attend(): pl.pallas_call(attend_kernel, out_shape=jax.ShapeDtypeStruct((tokens, wid...  3.97 us
    unnamed x7, local copies, waits for them, and re-layouts  2.83 us

profile of v2, /device:TPU:3, one launch (start us, length us, event | category | flops | bytes accessed | tf_op | source)
XLA Modules:
  0.0 61.1 jit_solution(5561849396431931215)
XLA Ops:
  0.6 0.0 copy-start.2
  0.6 0.0 copy-start
  0.7 53.7 %shard_map.104 = (bf16[128,2048]{1,0:T(8,128)(2,1)}, bf16[256,512]{1,0:T(8,128)(2,1)}) custom-call(bf16[128,1280]{1,0:T(8,128)(2,1)} %image_ref.1, f32[1280]{0:T(1024)} %gain_ref.1, s32[1,8,32]{2,1,0:T(8,128)} %want_ref.1, bf16[1280,1280]{1,0:T(8,128)(2,1)} %expand_any.1, bf16[1280,1280]{1,0:T(8,128)(2,1)} %shrink_any.1, bf16[1280,2048]{1,0:T(8,128)(2,1)} %proj_any.1, ...), custom_call_target="tpu_custom_call" | custom-call | tf_op jit(solution)/shard_map/pallas_call | solution.py:329
  54.3 0.0 copy-done.2
  54.3 0.0 copy-done
  54.3 0.0 copy-start.1
  54.3 0.9 %copy-done.1 = bf16[256,512]{1,0:T(8,128)(2,1)S(1)} copy-done((bf16[256,512]{1,0:T(8,128)(2,1)S(1)}, bf16[256,512]{1,0:T(8,128)(2,1)}, u32[]{:S(2)}) %copy-start.1) | copy-done | bytes 262168
  55.3 4.0 %shard_map.105 = bf16[256,2048]{1,0:T(8,128)(2,1)} custom-call(s32[2,4]{1,0:T(2,128)S(1)} %copy-done.2, bf16[256,2048]{1,0:T(8,128)(2,1)S(1)} %copy-done, bf16[256,512]{1,0:T(8,128)(2,1)S(1)} %copy-done.1), custom_call_target="tpu_custom_call" | custom-call | flops 536870912 | bytes 2097152 | tf_op jit(solution)/shard_map/pallas_call | solution.py:66
  59.3 1.9 %copy.12 = bf16[128,2048]{1,0:T(8,128)(2,1)} copy(bf16[128,2048]{1,0:T(8,128)(2,1)} %get-tuple-element.8) | data formatting | bytes 1048576
Async XLA Ops:
  0.6 53.7 %copy-start.2 = (s32[2,4]{1,0:T(2,128)S(1)}, s32[2,4]{1,0:T(2,128)}, u32[]{:S(2)}) copy-start(s32[2,4]{1,0:T(2,128)} %mask_ref.1) | copy-start | bytes 100
  0.6 53.7 %copy-start = (bf16[256,2048]{1,0:T(8,128)(2,1)S(1)}, bf16[256,2048]{1,0:T(8,128)(2,1)}, u32[]{:S(2)}) copy-start(bf16[256,2048]{1,0:T(8,128)(2,1)} %q_ref.1) | copy-start | bytes 3145732
  54.3 1.0 %copy-start.1 = (bf16[256,512]{1,0:T(8,128)(2,1)S(1)}, bf16[256,512]{1,0:T(8,128)(2,1)}, u32[]{:S(2)}) copy-start(bf16[256,512]{1,0:T(8,128)(2,1)} %get-tuple-element.5.kv_ref) | copy-start | bytes 786436

commit v3 on v2

--- a/solution.py
+++ b/solution.py
@@ -27,7 +27,12 @@
     return picked.reshape(wanted.shape + (row_data.shape[1],))
 
 
-def attend_kernel(mask_ref, q_ref, kv_ref, o_ref):
+def attend_kernel(moves, mask_ref, q_any, kv_ref, *refs):
+    if moves:
+        carried, o_ref, carried_out, q_ref, q_sem, carry_sem = refs
+        carry = pltpu.make_async_copy(carried, carried_out, carry_sem)
+    else:
+        o_ref, q_ref, q_sem = refs
     tokens, width = q_ref.shape
     slots = kv_ref.shape[0]
     groups = kv_ref.shape[1] // (2 * HDIM)
@@ -35,48 +40,67 @@
     tile_rows = slots // MAX_TILES
     scale = 1.0 / math.sqrt(HDIM)
     blocks = mask_ref.shape[0]
+    n_cut = width // (2 * HDIM)
+    loads = []
+    for n in range(n_cut):
+        cols = pl.ds(n * 2 * HDIM, 2 * HDIM)
+        loads.append(pltpu.make_async_copy(q_any.at[:, cols], q_ref.at[:, cols], q_sem.at[n]))
+        loads[-1].start()
+    if moves:
+        carry.start()
     slot = lax.broadcasted_iota(jnp.int32, (QBLK, slots), 1)
+    sights = []
     for b in range(blocks):
         seen = jnp.zeros((QBLK, slots), jnp.float32)
         for tile in range(MAX_TILES):
             inside = (slot >= tile * tile_rows) & (slot < (tile + 1) * tile_rows)
             seen = jnp.where(inside, (mask_ref[b, tile] > 0).astype(jnp.float32), seen)
-        visible = seen > 0.0
-        rows = pl.ds(b * QBLK, QBLK)
-        for g in range(groups):
-            key_rows = kv_ref[:, g * 2 * HDIM:g * 2 * HDIM + HDIM]
-            value_rows = kv_ref[:, g * 2 * HDIM + HDIM:(g + 1) * 2 * HDIM]
-            for h in range(per_group):
-                cols = pl.ds((g * per_group + h) * HDIM, HDIM)
-                scores = lax.dot_general(
-                    q_ref[rows, cols], key_rows, (((1,), (1,)), ((), ())),
-                    preferred_element_type=jnp.float32) * scale
-                masked = jnp.where(visible, scores, -1e30)
-                top = jnp.max(masked, axis=1, keepdims=True)
-                weights = jnp.where(visible, jnp.exp(masked - top), 0.0)
-                total = jnp.sum(weights, axis=1, keepdims=True)
-                total = jnp.where(total > 0.0, total, 1.0)
-                probs = (weights / total).astype(jnp.bfloat16)
-                o_ref[rows, cols] = jnp.dot(
-                    probs, value_rows, preferred_element_type=jnp.float32).astype(jnp.bfloat16)
-
-
-def attend(queries, kv_slots, block_mask):
+        sights.append(seen > 0.0)
+    for h in range(groups * per_group):
+        if h % 2 == 0:
+            loads[h // 2].wait()
+        g = h // per_group
+        key_rows = kv_ref[:, g * 2 * HDIM:g * 2 * HDIM + HDIM]
+        value_rows = kv_ref[:, g * 2 * HDIM + HDIM:(g + 1) * 2 * HDIM]
+        cols = pl.ds(h * HDIM, HDIM)
+        for b in range(blocks):
+            rows = pl.ds(b * QBLK, QBLK)
+            scores = lax.dot_general(
+                q_ref[rows, cols], key_rows, (((1,), (1,)), ((), ())), preferred_element_type=jnp.float32)
+            masked = jnp.where(sights[b], scores, -1e30)
+            top = jnp.max(masked, axis=1, keepdims=True)
+            weights = jnp.exp((masked - top) * scale)
+            total = jnp.sum(weights, axis=1, keepdims=True)
+            inverse = jnp.where(top > -1e29, 1.0 / total, 0.0)
+            summed = jnp.dot(weights.astype(jnp.bfloat16), value_rows, preferred_element_type=jnp.float32)
+            o_ref[rows, cols] = (summed * inverse).astype(jnp.bfloat16)
+    if moves:
+        carry.wait()
+
+
+def attend(queries, kv_slots, block_mask, carried=None):
     tokens, width = queries.shape
+    moves = carried is not None
+    anywhere = pl.BlockSpec(memory_space=pl.ANY)
+    vmem = pl.BlockSpec(memory_space=pltpu.VMEM)
+    shapes = [jax.ShapeDtypeStruct((tokens, width), jnp.bfloat16)]
+    operands = [block_mask, queries, kv_slots]
+    scratch = [pltpu.VMEM((tokens, width), jnp.bfloat16), pltpu.SemaphoreType.DMA((width // (2 * HDIM),))]
+    if moves:
+        shapes.append(jax.ShapeDtypeStruct(carried.shape, carried.dtype))
+        operands.append(carried)
+        scratch.append(pltpu.SemaphoreType.DMA)
     return pl.pallas_call(
-        attend_kernel,
-        out_shape=jax.ShapeDtypeStruct((tokens, width), jnp.bfloat16),
-        in_specs=[
-            pl.BlockSpec(memory_space=pltpu.SMEM),
-            pl.BlockSpec(memory_space=pltpu.VMEM),
-            pl.BlockSpec(memory_space=pltpu.VMEM),
-        ],
-        out_specs=pl.BlockSpec(memory_space=pltpu.VMEM),
+        functools.partial(attend_kernel, moves),
+        out_shape=tuple(shapes),
+        in_specs=[pl.BlockSpec(memory_space=pltpu.SMEM), anywhere, vmem] + [anywhere] * moves,
+        out_specs=tuple([vmem] + [anywhere] * moves),
+        scratch_shapes=scratch,
         cost_estimate=pl.CostEstimate(
             flops=4 * tokens * kv_slots.shape[0] * width, bytes_accessed=4 * tokens * width,
             transcendentals=tokens * kv_slots.shape[0] * width // HDIM),
-        compiler_params=pltpu.CompilerParams(vmem_limit_bytes=24 * 1024 * 1024),
-    )(block_mask, queries, kv_slots)
+        compiler_params=pltpu.CompilerParams(vmem_limit_bytes=60 * 1024 * 1024),
+    )(*operands)
 
 
 MESH = pl.DeviceIdType.MESH
@@ -142,15 +166,73 @@
     own_fold = fold_half(c)
     arrive(pair_in, a_r)
     own_fold += pair_in[...].astype(jnp.float32)
-    cross_out[...] = own_fold.astype(jnp.bfloat16)
+    for ch in range(2):
+        cross_out[ch] = own_fold[ch * depth:(ch + 1) * depth, :].astype(jnp.bfloat16)
     holds = z // 2 == x
-
-    def cross():
-        return remote(cross_out, cross_in, c_s, c_r, (s, over))
-
-    @pl.when(z // 2 != x)
+    passes = z // 2 != x
+
+    def cross(ch):
+        return remote(cross_out.at[ch], cross_in.at[ch], c_s.at[ch], c_r.at[ch], (s, over))
+
+    @pl.when(passes)
     def _():
-        cross().start()
+        for ch in range(2):
+            cross(ch).start()
+
+    def place(zl, yy, ch):
+        return (zl * 2 + yy) * 2 + ch
+
+    def up(i):
+        return remote(gathered.at[i], gathered.at[i], up_s.at[i], g_r.at[i], (s + 2, t))
+
+    def down(i):
+        return remote(gathered.at[i], gathered.at[i], down_s.at[i], g_r.at[i], (s - 2, t))
+
+    def across(i):
+        return remote(gathered.at[i], gathered.at[i], y_s.at[i], g_r.at[i], (2 * z + 1 - y, t))
+
+    def hand(i, k):
+        return remote(gathered.at[i], other.at[k], x_s.at[i], m_r.at[k], (s, core))
+
+    def hand_on(zl, yy, ch):
+        @pl.when(zl != c)
+        def _():
+            hand(place(zl, yy, ch), 2 * yy + ch).start()
+
+    def relay(zl, ch):
+        i = place(zl, y, ch)
+        zz = 2 * x + zl
+
+        @pl.when(z != zz)
+        def _():
+            arrive(gathered.at[i], g_r.at[i])
+
+        @pl.when((z >= zz) & (z < last))
+        def _():
+            up(i).start()
+
+        @pl.when((z <= zz) & (z > 0))
+        def _():
+            down(i).start()
+
+        across(i).start()
+        hand_on(zl, y, ch)
+
+    def y_relay(zl, ch):
+        i = place(zl, 1 - y, ch)
+        arrive(gathered.at[i], g_r.at[i])
+        hand_on(zl, 1 - y, ch)
+
+    first = (z + 2 * (1 - x)) // last
+    second = 1 - first
+
+    def begin(ch):
+        @pl.when(holds)
+        def _():
+            arrive(cross_in.at[ch], c_r.at[ch])
+            gathered[place(first, y, ch)] = (
+                cross_out[ch].astype(jnp.float32) + cross_in[ch].astype(jnp.float32)).astype(jnp.bfloat16)
+            relay(first, ch)
 
     values = image_ref[...].astype(jnp.float32)
     center = values - jnp.mean(values, axis=1, keepdims=True)
@@ -159,6 +241,7 @@
     loads[3].wait()
     wide = jnp.dot(normed, expand_ref[...], preferred_element_type=jnp.float32)
     hidden = (0.5 * wide * (1.0 + lax.erf(wide * math.sqrt(0.5)))).astype(jnp.bfloat16)
+    begin(0)
     loads[4].wait()
     partial = jnp.dot(hidden, shrink_ref[...], preferred_element_type=jnp.float32)
     for q in range(n_tp):
@@ -168,61 +251,7 @@
         peer = lax.rem(t + j, n_tp)
         go(remote(parts.at[peer], parts_in.at[j], b_s.at[j], b_r.at[j], (s, peer)))
 
-    def place(zl, yy, ch):
-        return (zl * 2 + yy) * 2 + ch
-
-    def up(i):
-        return remote(gathered.at[i], gathered.at[i], up_s.at[i], g_r.at[i], (s + 2, t))
-
-    def down(i):
-        return remote(gathered.at[i], gathered.at[i], down_s.at[i], g_r.at[i], (s - 2, t))
-
-    def across(i):
-        return remote(gathered.at[i], gathered.at[i], y_s.at[i], g_r.at[i], (2 * z + 1 - y, t))
-
-    def hand(i, k):
-        return remote(gathered.at[i], other.at[k], x_s.at[i], m_r.at[k], (s, core))
-
-    def hand_on(zl, yy, ch):
-        @pl.when(zl != c)
-        def _():
-            hand(place(zl, yy, ch), 2 * yy + ch).start()
-
-    def relay(zl, ch):
-        i = place(zl, y, ch)
-        zz = 2 * x + zl
-
-        @pl.when(z != zz)
-        def _():
-            arrive(gathered.at[i], g_r.at[i])
-
-        @pl.when((z >= zz) & (z < last))
-        def _():
-            up(i).start()
-
-        @pl.when((z <= zz) & (z > 0))
-        def _():
-            down(i).start()
-
-        across(i).start()
-        hand_on(zl, y, ch)
-
-    def y_relay(zl, ch):
-        i = place(zl, 1 - y, ch)
-        arrive(gathered.at[i], g_r.at[i])
-        hand_on(zl, 1 - y, ch)
-
-    first = (z + 2 * (1 - x)) // last
-    second = 1 - first
-
-    @pl.when(holds)
-    def _():
-        arrive(cross_in, c_r)
-        for ch in range(2):
-            rows = slice(ch * depth, (ch + 1) * depth)
-            gathered[place(first, y, ch)] = (
-                cross_out[rows, :].astype(jnp.float32) + cross_in[rows, :].astype(jnp.float32)).astype(jnp.bfloat16)
-            relay(first, ch)
+    begin(1)
 
     share = parts[t].astype(jnp.float32)
     for j in range(1, n_tp):
@@ -242,10 +271,15 @@
     go(remote(shares.at[t], shares.at[t], v_s.at[1], v_r.at[t], (s, core)))
     go(remote(shares.at[t], shares.at[t], v_s.at[2], v_r.at[t], (s, over)))
 
-    @pl.when(z // 2 != x)
+    @pl.when(passes)
     def _():
         for ch in range(2):
             relay(first, ch)
+
+    @pl.when(holds)
+    def _():
+        for ch in range(2):
+            relay(second, ch)
 
     for j in range(1, n_seq):
         peer = lax.rem(s + j, n_seq)
@@ -254,10 +288,11 @@
     go(remote(slots.at[t], slots.at[t], f_s.at[2], f_r.at[t], (s, over)))
     arrive(shares.at[over], v_r.at[over])
     go(remote(shares.at[over], shares.at[over], v_s.at[3], v_r.at[over], (s, core)))
-    relay(second, 0)
-    y_relay(first, 0)
-    relay(second, 1)
-    y_relay(first, 1)
+    for ch in range(2):
+        @pl.when(passes)
+        def _():
+            relay(second, ch)
+        y_relay(first, ch)
     arrive(slots.at[over], f_r.at[over])
     go(remote(slots.at[over], slots.at[over], f_s.at[3], f_r.at[over], (s, core)))
 
@@ -293,9 +328,10 @@
     for copy in sent:
         copy.wait_send()
 
-    @pl.when(z // 2 != x)
+    @pl.when(passes)
     def _():
-        cross().wait_send()
+        for ch in range(2):
+            cross(ch).wait_send()
 
     for zl in range(2):
         zz = 2 * x + zl
@@ -339,8 +375,8 @@
             pltpu.VMEM(kv_weight.shape, bf16),
             pltpu.VMEM((2 * depth, width), bf16),
             pltpu.VMEM((2 * depth, width), bf16),
-            pltpu.VMEM((2 * depth, width), bf16),
-            pltpu.VMEM((2 * depth, width), bf16),
+            pltpu.VMEM((2, depth, width), bf16),
+            pltpu.VMEM((2, depth, width), bf16),
             pltpu.VMEM((8, depth, width), bf16),
             pltpu.VMEM((4, depth, width), bf16),
             pltpu.VMEM((n_tp, rows, depth), bf16),
@@ -349,7 +385,7 @@
             pltpu.VMEM((n_tp, rows, depth), bf16),
             pltpu.VMEM((n_seq, cap, depth), bf16),
             pltpu.VMEM((n_tp, n_seq, cap, depth), bf16),
-            dma((5,)), dma, dma, dma, dma, dma((n_tp,)), dma((n_tp,)),
+            dma((5,)), dma, dma, dma((2,)), dma((2,)), dma((n_tp,)), dma((n_tp,)),
             dma((8,)), dma((8,)), dma((8,)), dma((8,)), dma((8,)), dma((4,)),
             dma((n_tp,)), dma((n_tp,)), dma((n_seq,)), dma((n_seq,)), dma((n_tp,)), dma((n_tp,)),
         ],
@@ -374,7 +410,8 @@
     if n_seq == 8 and n_tp == 4 and kv_weight.shape[1] == 2 * HDIM and wanted.shape[1] % 16 == 0:
         states, kv_slots = exchange(
             n_seq, n_tp, image_rows, norm_gain, send_list, expand_weight, shrink_weight, projector, kv_weight)
-        return (states, attend(queries, kv_slots, block_mask))
+        context, states = attend(queries, kv_slots, block_mask, states)
+        return (states, context)
     fold_part = jnp.dot(projector, kv_weight, preferred_element_type=jnp.float32).astype(jnp.bfloat16)
     fold_rows = lax.psum_scatter(fold_part, "tp", scatter_dimension=0, tiled=True)
     fold_rows = lax.all_gather(fold_rows, "seq", axis=1, tiled=True)
@@ -396,7 +433,7 @@
     slot_rows = arrived.reshape(-1, share_width)
     kv_part = jnp.dot(slot_rows, fold_rows, preferred_element_type=jnp.float32).astype(jnp.bfloat16)
     kv_slots = lax.psum_scatter(kv_part, "tp", scatter_dimension=1, tiled=True)
-    return (states, attend(queries, kv_slots, block_mask))
+    return (states, attend(queries, kv_slots, block_mask)[0])
 
 
 def solution(mesh):

time: 61.3 us -> 68.6 us (1.12)
  Pallas kernels: 57.6 us -> 67.8 us
  local copies, waits for them, and re-layouts: 2.83 us -> 0 us
    pallas_call x1, Pallas kernels: 3.97 us -> 19 us  [attend(): pl.pallas_call(functools.partial(attend_kernel, moves), out_shape=tuple(s...]
    pallas_call x1, Pallas kernels: 53.7 us -> 48.8 us  [exchange(): pl.pallas_call(functools.partial(exchange_kernel, n_seq, n_tp), out_shape...]
    unnamed x7 -> x0, local copies, waits for them, and re-layouts: 2.83 us -> none
where the time goes in v3:
time: 68.6 us; the launch traced here: 68.4 us
  Pallas kernels  67.8 us (99%)
    pallas_call x1, Pallas kernels, exchange(): pl.pallas_call(functools.partial(exchange_kernel, n_seq, n_tp), out_shape...  48.8 us
    pallas_call x1, Pallas kernels, attend(): pl.pallas_call(functools.partial(attend_kernel, moves), out_shape=tuple(s...  19 us

profile of v3, /device:TPU:3, one launch (start us, length us, event | category | flops | bytes accessed | tf_op | source)
XLA Modules:
  0.0 68.4 jit_solution(14025823359155576242)
XLA Ops:
  0.6 48.8 %shard_map.104 = (bf16[128,2048]{1,0:T(8,128)(2,1)}, bf16[256,512]{1,0:T(8,128)(2,1)}) custom-call(bf16[128,1280]{1,0:T(8,128)(2,1)} %image_ref.1, f32[1280]{0:T(1024)} %gain_ref.1, s32[1,8,32]{2,1,0:T(8,128)} %want_ref.1, bf16[1280,1280]{1,0:T(8,128)(2,1)} %expand_any.1, bf16[1280,1280]{1,0:T(8,128)(2,1)} %shrink_any.1, bf16[1280,2048]{1,0:T(8,128)(2,1)} %proj_any.1, ...), custom_call_target="tpu_custom_call" | custom-call | tf_op jit(solution)/shard_map/pallas_call | solution.py:365
  49.4 19.0 %shard_map.105 = (bf16[256,2048]{1,0:T(8,128)(2,1)}, bf16[128,2048]{1,0:T(8,128)(2,1)}) custom-call(s32[2,4]{1,0:T(2,128)} %mask_ref.1, bf16[256,2048]{1,0:T(8,128)(2,1)} %q_any.1, bf16[256,512]{1,0:T(8,128)(2,1)} %get-tuple-element.6.kv_ref, bf16[128,2048]{1,0:T(8,128)(2,1)} %get-tuple-element.7.refs_0_), custom_call_target="tpu_custom_call" | custom-call | flops 536870912 | bytes 2097152 | tf_op jit(solution)/shard_map/pallas_call | solution.py:93

commit v4 on v3

--- a/solution.py
+++ b/solution.py
@@ -27,12 +27,14 @@
     return picked.reshape(wanted.shape + (row_data.shape[1],))
 
 
-def attend_kernel(moves, mask_ref, q_any, kv_ref, *refs):
+def attend_kernel(moves, mask_ref, q_ref, kv_ref, *refs):
     if moves:
-        carried, o_ref, carried_out, q_ref, q_sem, carry_sem = refs
-        carry = pltpu.make_async_copy(carried, carried_out, carry_sem)
+        carried, o_ref, carried_out, held, carry_sem = refs
+        carry_in = pltpu.make_async_copy(carried, held, carry_sem.at[0])
+        carry_out = pltpu.make_async_copy(held, carried_out, carry_sem.at[1])
+        carry_in.start()
     else:
-        o_ref, q_ref, q_sem = refs
+        o_ref, = refs
     tokens, width = q_ref.shape
     slots = kv_ref.shape[0]
     groups = kv_ref.shape[1] // (2 * HDIM)
@@ -40,14 +42,6 @@
     tile_rows = slots // MAX_TILES
     scale = 1.0 / math.sqrt(HDIM)
     blocks = mask_ref.shape[0]
-    n_cut = width // (2 * HDIM)
-    loads = []
-    for n in range(n_cut):
-        cols = pl.ds(n * 2 * HDIM, 2 * HDIM)
-        loads.append(pltpu.make_async_copy(q_any.at[:, cols], q_ref.at[:, cols], q_sem.at[n]))
-        loads[-1].start()
-    if moves:
-        carry.start()
     slot = lax.broadcasted_iota(jnp.int32, (QBLK, slots), 1)
     sights = []
     for b in range(blocks):
@@ -57,8 +51,9 @@
             seen = jnp.where(inside, (mask_ref[b, tile] > 0).astype(jnp.float32), seen)
         sights.append(seen > 0.0)
     for h in range(groups * per_group):
-        if h % 2 == 0:
-            loads[h // 2].wait()
+        if moves and h == groups * per_group // 2:
+            carry_in.wait()
+            carry_out.start()
         g = h // per_group
         key_rows = kv_ref[:, g * 2 * HDIM:g * 2 * HDIM + HDIM]
         value_rows = kv_ref[:, g * 2 * HDIM + HDIM:(g + 1) * 2 * HDIM]
@@ -75,7 +70,7 @@
             summed = jnp.dot(weights.astype(jnp.bfloat16), value_rows, preferred_element_type=jnp.float32)
             o_ref[rows, cols] = (summed * inverse).astype(jnp.bfloat16)
     if moves:
-        carry.wait()
+        carry_out.wait()
 
 
 def attend(queries, kv_slots, block_mask, carried=None):
@@ -85,15 +80,15 @@
     vmem = pl.BlockSpec(memory_space=pltpu.VMEM)
     shapes = [jax.ShapeDtypeStruct((tokens, width), jnp.bfloat16)]
     operands = [block_mask, queries, kv_slots]
-    scratch = [pltpu.VMEM((tokens, width), jnp.bfloat16), pltpu.SemaphoreType.DMA((width // (2 * HDIM),))]
+    scratch = []
     if moves:
         shapes.append(jax.ShapeDtypeStruct(carried.shape, carried.dtype))
         operands.append(carried)
-        scratch.append(pltpu.SemaphoreType.DMA)
+        scratch += [pltpu.VMEM(carried.shape, carried.dtype), pltpu.SemaphoreType.DMA((2,))]
     return pl.pallas_call(
         functools.partial(attend_kernel, moves),
         out_shape=tuple(shapes),
-        in_specs=[pl.BlockSpec(memory_space=pltpu.SMEM), anywhere, vmem] + [anywhere] * moves,
+        in_specs=[pl.BlockSpec(memory_space=pltpu.SMEM), vmem, vmem] + [anywhere] * moves,
         out_specs=tuple([vmem] + [anywhere] * moves),
         scratch_shapes=scratch,
         cost_estimate=pl.CostEstimate(

time: 68.6 us -> 54.2 us (0.79)
  Pallas kernels: 67.8 us -> 53.4 us
    pallas_call x1, Pallas kernels: 19 us -> 4.56 us  [attend(): pl.pallas_call(functools.partial(attend_kernel, moves), out_shape=tuple(s...]
where the time goes in v4:
time: 54.2 us; the launch traced here: 54 us
  Pallas kernels  53.4 us (99%)
  between operations  0.64 us (1%)
    pallas_call x1, Pallas kernels, exchange(): pl.pallas_call(functools.partial(exchange_kernel, n_seq, n_tp), out_shape...  48.8 us
    pallas_call x1, Pallas kernels, attend(): pl.pallas_call(functools.partial(attend_kernel, moves), out_shape=tuple(s...  4.56 us

profile of v4, /device:TPU:3, one launch (start us, length us, event | category | flops | bytes accessed | tf_op | source)
XLA Modules:
  0.0 54.0 jit_solution(13820590844634663937)
XLA Ops:
  0.6 48.8 %shard_map.104 = (bf16[128,2048]{1,0:T(8,128)(2,1)}, bf16[256,512]{1,0:T(8,128)(2,1)}) custom-call(bf16[128,1280]{1,0:T(8,128)(2,1)} %image_ref.1, f32[1280]{0:T(1024)} %gain_ref.1, s32[1,8,32]{2,1,0:T(8,128)} %want_ref.1, bf16[1280,1280]{1,0:T(8,128)(2,1)} %expand_any.1, bf16[1280,1280]{1,0:T(8,128)(2,1)} %shrink_any.1, bf16[1280,2048]{1,0:T(8,128)(2,1)} %proj_any.1, ...), custom_call_target="tpu_custom_call" | custom-call | tf_op jit(solution)/shard_map/pallas_call | solution.py:360
  49.4 4.6 %shard_map.105 = (bf16[256,2048]{1,0:T(8,128)(2,1)}, bf16[128,2048]{1,0:T(8,128)(2,1)}) custom-call(s32[2,4]{1,0:T(2,128)} %mask_ref.1, bf16[256,2048]{1,0:T(8,128)(2,1)} %q_ref.1, bf16[256,512]{1,0:T(8,128)(2,1)} %get-tuple-element.6.kv_ref, bf16[128,2048]{1,0:T(8,128)(2,1)} %get-tuple-element.7.refs_0_), custom_call_target="tpu_custom_call" | custom-call | flops 536870912 | bytes 2097152 | tf_op jit(solution)/shard_map/pallas_call | solution.py:88

commit v5 on v4

--- a/solution.py
+++ b/solution.py
@@ -302,11 +302,12 @@
             term = jnp.dot(shares[q], proj_ref[q * depth:(q + 1) * depth, cols], preferred_element_type=jnp.float32)
             total = term if total is None else total + term
         states_ref[:, cols] = total.astype(jnp.bfloat16)
+        if n == 1:
+            y_relay(second, 0)
 
     arrive(slots.at[core], f_r.at[core])
     arrive(slots.at[skew], f_r.at[skew])
-    for ch in range(2):
-        y_relay(second, ch)
+    y_relay(second, 1)
     width = kvw_ref.shape[1]
     for yy in range(2):
         total = None

time: 54.2 us -> 54.2 us (level)
  no operation moved by 1% of the time
where the time goes in v5:
time: 54.2 us; the launch traced here: 54 us
  Pallas kernels  53.4 us (99%)
  between operations  0.64 us (1%)
    pallas_call x1, Pallas kernels, exchange(): pl.pallas_call(functools.partial(exchange_kernel, n_seq, n_tp), out_shape...  48.8 us
    pallas_call x1, Pallas kernels, attend(): pl.pallas_call(functools.partial(attend_kernel, moves), out_shape=tuple(s...  4.56 us

profile of v5, /device:TPU:3, one launch (start us, length us, event | category | flops | bytes accessed | tf_op | source)
XLA Modules:
  0.0 54.0 jit_solution(11760652838008049015)
XLA Ops:
  0.6 48.8 %shard_map.104 = (bf16[128,2048]{1,0:T(8,128)(2,1)}, bf16[256,512]{1,0:T(8,128)(2,1)}) custom-call(bf16[128,1280]{1,0:T(8,128)(2,1)} %image_ref.1, f32[1280]{0:T(1024)} %gain_ref.1, s32[1,8,32]{2,1,0:T(8,128)} %want_ref.1, bf16[1280,1280]{1,0:T(8,128)(2,1)} %expand_any.1, bf16[1280,1280]{1,0:T(8,128)(2,1)} %shrink_any.1, bf16[1280,2048]{1,0:T(8,128)(2,1)} %proj_any.1, ...), custom_call_target="tpu_custom_call" | custom-call | tf_op jit(solution)/shard_map/pallas_call | solution.py:361
  49.4 4.6 %shard_map.105 = (bf16[256,2048]{1,0:T(8,128)(2,1)}, bf16[128,2048]{1,0:T(8,128)(2,1)}) custom-call(s32[2,4]{1,0:T(2,128)} %mask_ref.1, bf16[256,2048]{1,0:T(8,128)(2,1)} %q_ref.1, bf16[256,512]{1,0:T(8,128)(2,1)} %get-tuple-element.6.kv_ref, bf16[128,2048]{1,0:T(8,128)(2,1)} %get-tuple-element.7.refs_0_), custom_call_target="tpu_custom_call" | custom-call | flops 536870912 | bytes 2097152 | tf_op jit(solution)/shard_map/pallas_call | solution.py:88
